TPU v7x, 128 devices: a whole 4x4x4 slice. The times are simulated.
128 devices in a mesh: row: 8 (over y, core), col: 16 (over z, x).
Axes of the slice: x: 4, y: 4, z: 4, core: 2. Of those that a mesh axis runs over, the one named last changes fastest.
Arguments:
- inputs: bfloat16 [1280, 6144], P('col', 'row'), may hold values from -6 to 6
- w_in: bfloat16 [6144, 24576], P('row', 'col'), may hold values from -0.078125 to 0.078125
- b_in: float32 [24576], P('col'), may hold values from -3 to 3
- w_out: bfloat16 [24576, 6144], P('col', 'row'), may hold values from -0.0390625 to 0.0390625
- b_out: float32 [6144], P('row'), may hold values from -3 to 3
- out_grad: bfloat16 [1280, 6144], P('col', 'row'), may hold values from -0.625 to 0.625
Outputs:
- output: bfloat16 [1280, 6144], P('col', 'row')
- input_grad: bfloat16 [1280, 6144], P('col', 'row')
- w_in_grad: float32 [6144, 24576], P('row', 'col')
- b_in_grad: float32 [24576], P('col')
- w_out_grad: float32 [24576, 6144], P('col', 'row')
- b_out_grad: float32 [6144], P('row')
All inputs are finite; a program needn't handle non-finite values.
Results may differ from a plain program's by a relative error of at most 0.007.
Values may be sent and summed in bfloat16 or wider, within the bound.
A program may use at most 128 MiB of HBM per device.

v0:
```python
import jax
import jax.numpy as jnp
from jax import lax
from jax.sharding import PartitionSpec as P


def gelu_parts(hidden):
    half = 0.5 * (1.0 + jax.scipy.special.erf(hidden * 0.7071067811865476))
    slope = half + hidden * jnp.exp(-0.5 * hidden * hidden) * 0.3989422804014327
    return (hidden * half, slope)


def shards(inputs, w_in, b_in, w_out, b_out, out_grad):
    inputs_all, grad_all = (
        lax.all_gather(inputs, "col", axis=0, tiled=True),
        lax.all_gather(out_grad, "col", axis=0, tiled=True),
    )
    partial_value = jnp.dot(inputs_all, w_in, preferred_element_type=jnp.float32)
    hidden = lax.psum(partial_value, "row") + b_in
    act, slope = gelu_parts(hidden)
    act_all = act.astype(jnp.bfloat16)
    rows = act_all
    output = (
        lax.psum_scatter(
            jnp.dot(rows, w_out, preferred_element_type=jnp.float32),
            "col",
            scatter_dimension=0,
            tiled=True,
        )
        + b_out
    ).astype(jnp.bfloat16)
    b_out_grad = jnp.sum(grad_all, axis=0, dtype=jnp.float32)
    w_out_grad = jnp.einsum("tf,td->fd", act_all, grad_all, preferred_element_type=jnp.float32)
    partial_grad = jnp.einsum("td,fd->tf", grad_all, w_out, preferred_element_type=jnp.float32)
    act_grad = lax.psum(partial_grad, "row")
    pre_grad = (act_grad * slope).astype(jnp.bfloat16)
    b_in_grad = jnp.sum(pre_grad, axis=0, dtype=jnp.float32)
    w_in_grad = jnp.einsum("td,tf->df", inputs_all, pre_grad, preferred_element_type=jnp.float32)
    rows = pre_grad
    input_grad = lax.psum_scatter(
        jnp.einsum("tf,df->td", rows, w_in, preferred_element_type=jnp.float32),
        "col",
        scatter_dimension=0,
        tiled=True,
    ).astype(jnp.bfloat16)
    return (output, input_grad, w_in_grad, b_in_grad, w_out_grad, b_out_grad)


def solution(mesh):
    placed = (
        P("col", "row"),
        P("row", "col"),
        P("col"),
        P("col", "row"),
        P("row"),
        P("col", "row"),
    )
    return jax.shard_map(
        shards,
        mesh=mesh,
        in_specs=placed,
        out_specs=(
            P("col", "row"),
            P("col", "row"),
            P("row", "col"),
            P("col"),
            P("col", "row"),
            P("row"),
        ),
        check_vma=False,
    )
```

profile of v0, /device:TPU:0, one launch (start us, length us, event | category | flops | bytes accessed | tf_op | source)
XLA Modules:
  0.0 465.8 jit_solution(393771307948937727)
XLA Ops:
  7.2 0.0 copy-start
  7.2 0.0 all-gather.5.cloned.1.call-start
  7.2 0.7 all-gather.5.cloned.1.call-update
  7.9 0.0 all-gather.3.cloned.1.call-start
  8.0 0.7 all-gather.3.cloned.1.call-update
  8.7 0.0 all-reduce.3.cloned.1.call-start
  8.7 48.7 %all-gather.5.cloned.1.call-done = bf16[1280,768]{1,0:T(8,128)(2,1)} async-done(((bf16[80,768]{1,0:T(8,128)(2,1)}), bf16[1280,768]{1,0:T(8,128)(2,1)}) %all-gather.5.cloned.1.call-update) | async-done | bytes 1966096 | tf_op jit(solution)/shard_map/all_gather | solution.py:16
  57.4 8.7 %fusion.9 = f32[1280,1536]{1,0:T(8,128)} fusion(bf16[1280,768]{1,0:T(8,128)(2,1)} %all-gather.5.cloned.1.call-done, bf16[1536,768]{1,0:T(8,128)(2,1)} %param.9), kind=kOutput, calls=%fused_computation.15 | convolution fusion | flops 3019898880 | bytes 12189696 | tf_op jit(solution)/shard_map/td,fd->tf/dot_general | solution.py:34
  66.1 37.5 %all-gather.3.cloned.1.call-done = bf16[1280,768]{1,0:T(8,128)(2,1)} async-done(((bf16[80,768]{1,0:T(8,128)(2,1)}), bf16[1280,768]{1,0:T(8,128)(2,1)}) %all-gather.3.cloned.1.call-update) | async-done | bytes 1966096 | tf_op jit(solution)/shard_map/all_gather | solution.py:15
  103.5 7.0 %fusion.7 = f32[1280,1536]{1,0:T(8,128)} fusion(bf16[1280,768]{1,0:T(8,128)(2,1)} %all-gather.3.cloned.1.call-done, bf16[768,1536]{1,0:T(8,128)(2,1)S(1)} %copy-done), kind=kOutput, calls=%fused_computation.13 | convolution fusion | flops 3019898880 | bytes 12189696 | tf_op jit(solution)/shard_map/dot_general | solution.py:18
  110.5 0.0 all-reduce.3.cloned.1.call-update
  110.5 0.0 reduce-scatter.5.cloned.1.call-start
  110.6 173.0 %all-reduce.3.cloned.1.call-done = (f32[1280,1536]{1,0:T(8,128)}, f32[1280,1536]{1,0:T(8,128)}) async-done(((f32[1280,1536]{1,0:T(8,128)}, f32[1280,1536]{1,0:T(8,128)}), (f32[1280,1536]{1,0:T(8,128)}, f32[1280,1536]{1,0:T(8,128)})) %all-reduce.3.cloned.1.call-update) | async-done | bytes 15728656 | tf_op jit(solution)/shard_map/psum | solution.py:19
  283.6 0.0 copy-done.4
  283.6 10.6 %convert_reduce_fusion = (f32[1536]{0:T(1024)}, bf16[1280,1536]{1,0:T(8,128)(2,1)S(1)}, bf16[1280,1536]{1,0:T(8,128)(2,1)}) fusion(f32[1280,1536]{1,0:T(8,128)} %get-tuple-element.13, f32[1280,1536]{1,0:T(8,128)} %get-tuple-element.12, f32[1536]{0:T(1024)S(1)} %copy-done.4), kind=kLoop, calls=%fused_computation.7 | loop fusion | flops 29489664 | bytes 23605248 | tf_op jit(solution)/shard_map/reduce_sum | solution.py:37
  294.2 1.9 copy-done.2
  296.1 5.1 %fusion.10 = f32[1280,768]{1,0:T(8,128)} fusion(bf16[1280,1536]{1,0:T(8,128)(2,1)S(1)} %get-tuple-element.15, bf16[768,1536]{1,0:T(8,128)(2,1)S(1)} %copy-done), kind=kOutput, calls=%fused_computation.16 | convolution fusion | flops 3019898880 | bytes 10223616 | tf_op jit(solution)/shard_map/tf,df->td/dot_general | solution.py:41
  301.2 0.0 reduce-scatter.5.cloned.1.call-update
  301.3 0.2 reduce-scatter.3.cloned.1.call-start
  301.5 1.4 copy-done.6
  302.9 7.2 %fusion.8 = f32[1280,768]{1,0:T(8,128)} fusion(bf16[1280,1536]{1,0:T(8,128)(2,1)} %get-tuple-element.16, bf16[1536,768]{1,0:T(8,128)(2,1)S(1)} %copy-done.6), kind=kOutput, calls=%fused_computation.14 | convolution fusion | flops 3019898880 | bytes 10223616 | tf_op jit(solution)/shard_map/dot_general | solution.py:25
  310.1 0.0 reduce-scatter.3.cloned.1.call-update
  310.1 1.6 copy-done.3
  311.7 0.9 convert_reduce_fusion.1
  312.6 8.2 %convolution_bitcast_fusion = f32[768,1536]{0,1:T(8,128)} fusion(bf16[1280,1536]{1,0:T(8,128)(2,1)} %copy-done.2, bf16[1280,768]{1,0:T(8,128)(2,1)} %all-gather.3.cloned.1.call-done), kind=kOutput, calls=%fused_computation.11 | convolution fusion | flops 3019898880 | bytes 10616832 | tf_op jit(solution)/shard_map/td,tf->df/dot_general | solution.py:38
  320.8 6.1 %copy.12 = f32[768,1536]{1,0:T(8,128)} copy(f32[768,1536]{0,1:T(8,128)} %convolution_bitcast_fusion) | data formatting | bytes 9437184
  327.0 8.4 %fusion.11 = f32[1536,768]{1,0:T(8,128)} fusion(bf16[1280,1536]{1,0:T(8,128)(2,1)} %get-tuple-element.16, bf16[1280,768]{1,0:T(8,128)(2,1)} %all-gather.5.cloned.1.call-done), kind=kOutput, calls=%fused_computation.17 | convolution fusion | flops 3019898880 | bytes 10616832 | tf_op jit(solution)/shard_map/tf,td->fd/dot_general | solution.py:33
  335.4 42.9 %reduce-scatter.5.cloned.1.call-done = f32[80,768]{1,0:T(8,128)} async-done(((f32[1280,768]{1,0:T(8,128)}), f32[80,768]{1,0:T(8,128)}) %reduce-scatter.5.cloned.1.call-update) | async-done | bytes 245776 | tf_op jit(solution)/shard_map/reduce_scatter | solution.py:40
  378.3 1.6 convert_element_type.21
  379.9 77.8 %reduce-scatter.3.cloned.1.call-done = f32[80,768]{1,0:T(8,128)} async-done(((f32[1280,768]{1,0:T(8,128)}), f32[80,768]{1,0:T(8,128)}) %reduce-scatter.3.cloned.1.call-update) | async-done | bytes 245776 | tf_op jit(solution)/shard_map/reduce_scatter | solution.py:24
  457.7 0.0 copy-done.5
  457.7 1.6 add_convert_fusion
  (8 shorter events, 0.0 us)
Async XLA Ops:
  7.2 96.4 %copy-start = (bf16[768,1536]{1,0:T(8,128)(2,1)S(1)}, bf16[768,1536]{1,0:T(8,128)(2,1)}, u32[]{:S(2)}) copy-start(bf16[768,1536]{1,0:T(8,128)(2,1)} %param.7) | copy-start | bytes 7077892
  7.2 50.2 %all-gather.5.cloned.1.call-start = ((), (), s32[]{:S(2)}) async-start(), calls=%async_computation.4 | async-start | bytes 2088960 | tf_op jit(solution)/shard_map/all_gather | solution.py:16
  7.9 95.6 %all-gather.3.cloned.1.call-start = ((), (), s32[]{:S(2)}) async-start(), calls=%async_computation.2 | async-start | bytes 2088960 | tf_op jit(solution)/shard_map/all_gather | solution.py:15
  8.7 274.9 %all-reduce.3.cloned.1.call-start = ((), (), s32[]{:S(2)}) async-start(), calls=%async_computation.6 | async-start | bytes 31457280 | tf_op jit(solution)/shard_map/psum | solution.py:19
  110.5 173.1 %copy-start.4 = (f32[1536]{0:T(1024)S(1)}, f32[1536]{0:T(1024)}, u32[]{:S(2)}) copy-start(f32[1536]{0:T(1024)} %param.8) | copy-start | bytes 18436
  110.5 267.7 %reduce-scatter.5.cloned.1.call-start = ((), (), s32[]{:S(2)}) async-start(), calls=%async_computation.5 | async-start | bytes 4177920 | tf_op jit(solution)/shard_map/reduce_scatter | solution.py:40
  294.2 1.9 copy-start.2
  301.2 1.7 copy-start.6
  301.3 156.4 %reduce-scatter.3.cloned.1.call-start = ((), (), s32[]{:S(2)}) async-start(), calls=%async_computation.3 | async-start | bytes 4177920 | tf_op jit(solution)/shard_map/reduce_scatter | solution.py:24
  310.1 1.6 copy-start.3
  327.0 130.7 %copy-start.5 = (f32[768]{0:T(1024)S(1)}, f32[768]{0:T(1024)}, u32[]{:S(2)}) copy-start(f32[768]{0:T(1024)} %param.10) | copy-start | bytes 9220
  327.0 132.3 %copy-start.1 = (bf16[768,1536]{1,0:T(8,128)(2,1)S(1)}, bf16[768,1536]{1,0:T(8,128)(2,1)}, u32[]{:S(2)}) copy-start(bf16[768,1536]{1,0:T(8,128)(2,1)} %param.7) | copy-start | bytes 7077892
Sparse Core Ops, SparseCore 0:
  10.2 47.1 all-gather.4
  59.5 43.9 all-gather.2
  110.6 172.8 all-reduce.2
  301.4 76.8 reduce-scatter.4
  381.5 76.1 reduce-scatter.2
where the time goes:
time: 466 us
  waiting for transfers between devices  381 us (82%)
  matrix products  44.6 us (10%)
  other arithmetic  14.7 us (3%)
  between operations  13.8 us (3%)
  local copies, waits for them, and re-layouts  11 us (2%)
    psum x1, waiting for transfers between devices, shards(): hidden = lax.psum(partial_value, 'row') + b_in  173 us
    reduce_scatter x1, waiting for transfers between devices, shards(): lax.psum_scatter(jnp.dot(rows, w_out, preferred_element_type=jnp.float32)...  77.8 us
    all_gather x1, waiting for transfers between devices, shards(): lax.all_gather(out_grad, 'col', axis=0, tiled=True)  48.7 us
    reduce_scatter x1, waiting for transfers between devices, shards(): lax.psum_scatter(jnp.einsum('tf,df->td', rows, w_in, preferred_element_ty...  42.9 us
    all_gather x1, waiting for transfers between devices, shards(): lax.all_gather(inputs, 'col', axis=0, tiled=True)  37.5 us
    unnamed x15, local copies, waits for them, and re-layouts  11 us
    reduce_sum x1, other arithmetic, shards(): b_in_grad = jnp.sum(pre_grad, axis=0, dtype=jnp.float32)  10.6 us
  transfers between devices with their start and end apart: 5, of which 5 were waited for; matrix products, arithmetic and copies ran while one was open for 9% of the time, Pallas kernels for 0%

commit v1 on v0

--- a/solution.py
+++ b/solution.py
@@ -13,7 +13,9 @@
 def shards(inputs, w_in, b_in, w_out, b_out, out_grad):
     inputs_all, grad_all = (
         lax.all_gather(inputs, "col", axis=0, tiled=True),
-        lax.all_gather(out_grad, "col", axis=0, tiled=True),
+        jnp.concatenate(
+            lax.all_to_all(jnp.stack([out_grad] * lax.axis_size("col")), "col", 0, 0), axis=0
+        ),
     )
     partial_value = jnp.dot(inputs_all, w_in, preferred_element_type=jnp.float32)
     hidden = lax.psum(partial_value, "row") + b_in

time: 466 us -> 429 us (0.921)
  waiting for transfers between devices: 381 us -> 308 us
  blocking collectives: 0 us -> 36.7 us
    all_gather x1 -> x0, waiting for transfers between devices: 48.7 us -> none  [shards(): lax.all_gather(out_grad, 'col', axis=0, tiled=True)]
    all_to_all x0 -> x1, blocking collectives: none -> 36.7 us  [shards(): lax.all_to_all(jnp.stack([out_grad] * lax.axis_size('col')), 'col', 0, 0)]
    all_gather x1, waiting for transfers between devices: 37.5 us -> 13.1 us  [shards(): lax.all_gather(inputs, 'col', axis=0, tiled=True)]
    unnamed x15 -> x19, local copies, waits for them, and re-layouts: 11 us -> 12.3 us
  transfers between devices with their start and end apart: 5 -> 4, of which waited for: 5 -> 4; matrix products, arithmetic and copies ran while one was open for 9% -> 9% of each run, Pallas kernels for 0% -> 0%
where the time goes in v1:
time: 429 us; the launch traced here: 428 us
  waiting for transfers between devices  308 us (72%)
  matrix products  41.3 us (10%)
  blocking collectives  36.7 us (9%)
  other arithmetic  14.8 us (3%)
  between operations  13.8 us (3%)
  local copies, waits for them, and re-layouts  13.5 us (3%)
    psum x1, waiting for transfers between devices, shards(): hidden = lax.psum(partial_value, 'row') + b_in  173 us
    reduce_scatter x1, waiting for transfers between devices, shards(): lax.psum_scatter(jnp.dot(rows, w_out, preferred_element_type=jnp.float32)...  77.9 us
    reduce_scatter x1, waiting for transfers between devices, shards(): lax.psum_scatter(jnp.einsum('tf,df->td', rows, w_in, preferred_element_ty...  43 us
    all_to_all x1, blocking collectives, shards(): lax.all_to_all(jnp.stack([out_grad] * lax.axis_size('col')), 'col', 0, 0)  36.7 us
    all_gather x1, waiting for transfers between devices, shards(): lax.all_gather(inputs, 'col', axis=0, tiled=True)  13.1 us
    unnamed x19, local copies, waits for them, and re-layouts  12.3 us
    reduce_sum x1, other arithmetic, shards(): b_in_grad = jnp.sum(pre_grad, axis=0, dtype=jnp.float32)  10.6 us
  transfers between devices with their start and end apart: 4, of which 4 were waited for; matrix products, arithmetic and copies ran while one was open for 9% of the time, Pallas kernels for 0%

profile of v1, /device:TPU:0, one launch (start us, length us, event | category | flops | bytes accessed | tf_op | source)
XLA Modules:
  0.0 428.1 jit_solution(4999324123319837089)
XLA Ops:
  7.2 0.0 copy-start
  7.2 0.0 all-gather.2.cloned.1.call-start
  7.2 0.7 all-gather.2.cloned.1.call-update
  7.9 0.0 all-reduce.3.cloned.1.call-start
  8.0 0.0 copy-start.7
  8.0 1.2 stack.2
  9.2 36.7 %all_to_all.5 = bf16[16,80,768]{2,1,0:T(8,128)(2,1)S(1)} all-to-all(bf16[16,80,768]{2,1,0:T(8,128)(2,1)S(1)} %stack.2), channel_id=1, replica_groups=mesh['row'=8,'col'=16] {'col'}, dimensions={0} | all-to-all | bytes 3932160 | tf_op jit(solution)/shard_map/all_to_all | solution.py:17
  45.9 1.3 copy-done.2
  47.1 0.0 copy-done.7
  47.1 5.4 %fusion.9 = f32[1280,1536]{1,0:T(8,128)} fusion(bf16[1280,768]{1,0:T(8,128)(2,1)S(1)} %bitcast.15, bf16[1536,768]{1,0:T(8,128)(2,1)S(1)} %copy-done.7), kind=kOutput, calls=%fused_computation.15 | convolution fusion | flops 3019898880 | bytes 12189696 | tf_op jit(solution)/shard_map/td,fd->tf/dot_general | solution.py:36
  52.5 13.1 %all-gather.2.cloned.1.call-done = bf16[1280,768]{1,0:T(8,128)(2,1)} async-done(((bf16[80,768]{1,0:T(8,128)(2,1)}), bf16[1280,768]{1,0:T(8,128)(2,1)}) %all-gather.2.cloned.1.call-update) | async-done | bytes 1966096 | tf_op jit(solution)/shard_map/all_gather | solution.py:15
  65.6 6.9 %fusion.7 = f32[1280,1536]{1,0:T(8,128)} fusion(bf16[1280,768]{1,0:T(8,128)(2,1)} %all-gather.2.cloned.1.call-done, bf16[768,1536]{1,0:T(8,128)(2,1)S(1)} %copy-done), kind=kOutput, calls=%fused_computation.13 | convolution fusion | flops 3019898880 | bytes 12189696 | tf_op jit(solution)/shard_map/dot_general | solution.py:20
  72.5 0.0 all-reduce.3.cloned.1.call-update
  72.6 0.0 reduce-scatter.5.cloned.1.call-start
  72.6 173.0 %all-reduce.3.cloned.1.call-done = (f32[1280,1536]{1,0:T(8,128)}, f32[1280,1536]{1,0:T(8,128)}) async-done(((f32[1280,1536]{1,0:T(8,128)}, f32[1280,1536]{1,0:T(8,128)}), (f32[1280,1536]{1,0:T(8,128)}, f32[1280,1536]{1,0:T(8,128)})) %all-reduce.3.cloned.1.call-update) | async-done | bytes 15728656 | tf_op jit(solution)/shard_map/psum | solution.py:21
  245.6 10.6 %convert_reduce_fusion = (f32[1536]{0:T(1024)}, bf16[1280,1536]{1,0:T(8,128)(2,1)S(1)}, bf16[1280,1536]{1,0:T(8,128)(2,1)}) fusion(f32[1280,1536]{1,0:T(8,128)} %get-tuple-element.19, f32[1280,1536]{1,0:T(8,128)} %get-tuple-element.18, f32[1536]{0:T(1024)S(1)} %copy-done.5), kind=kLoop, calls=%fused_computation.7 | loop fusion | flops 29489664 | bytes 23605248 | tf_op jit(solution)/shard_map/reduce_sum | solution.py:39
  256.3 1.9 copy-done.4
  258.2 5.1 %fusion.10 = f32[1280,768]{1,0:T(8,128)} fusion(bf16[1280,1536]{1,0:T(8,128)(2,1)S(1)} %get-tuple-element.21, bf16[768,1536]{1,0:T(8,128)(2,1)S(1)} %copy-done), kind=kOutput, calls=%fused_computation.16 | convolution fusion | flops 3019898880 | bytes 10223616 | tf_op jit(solution)/shard_map/tf,df->td/dot_general | solution.py:43
  263.3 0.0 reduce-scatter.5.cloned.1.call-update
  263.3 0.2 reduce-scatter.3.cloned.1.call-start
  263.6 1.4 copy-done.8
  265.0 7.2 %fusion.8 = f32[1280,768]{1,0:T(8,128)} fusion(bf16[1280,1536]{1,0:T(8,128)(2,1)} %get-tuple-element.22, bf16[1536,768]{1,0:T(8,128)(2,1)S(1)} %copy-done.8), kind=kOutput, calls=%fused_computation.14 | convolution fusion | flops 3019898880 | bytes 10223616 | tf_op jit(solution)/shard_map/dot_general | solution.py:27
  272.2 0.0 reduce-scatter.3.cloned.1.call-update
  272.2 1.6 copy-done.3
  273.8 0.9 convert_reduce_fusion.1
  274.7 8.2 %convolution_bitcast_fusion = f32[768,1536]{0,1:T(8,128)} fusion(bf16[1280,1536]{1,0:T(8,128)(2,1)} %copy-done.4, bf16[1280,768]{1,0:T(8,128)(2,1)} %all-gather.2.cloned.1.call-done), kind=kOutput, calls=%fused_computation.11 | convolution fusion | flops 3019898880 | bytes 10616832 | tf_op jit(solution)/shard_map/td,tf->df/dot_general | solution.py:40
  282.9 6.1 %copy.13 = f32[768,1536]{1,0:T(8,128)} copy(f32[768,1536]{0,1:T(8,128)} %convolution_bitcast_fusion) | data formatting | bytes 9437184
  289.0 8.4 %fusion.11 = f32[1536,768]{1,0:T(8,128)} fusion(bf16[1280,1536]{1,0:T(8,128)(2,1)} %get-tuple-element.22, bf16[1280,768]{1,0:T(8,128)(2,1)} %bitcast.16), kind=kOutput, calls=%fused_computation.17 | convolution fusion | flops 3019898880 | bytes 10616832 | tf_op jit(solution)/shard_map/tf,td->fd/dot_general | solution.py:35
  297.5 43.0 %reduce-scatter.5.cloned.1.call-done = f32[80,768]{1,0:T(8,128)} async-done(((f32[1280,768]{1,0:T(8,128)}), f32[80,768]{1,0:T(8,128)}) %reduce-scatter.5.cloned.1.call-update) | async-done | bytes 245776 | tf_op jit(solution)/shard_map/reduce_scatter | solution.py:42
  340.5 1.6 convert_element_type.22
  342.1 77.9 %reduce-scatter.3.cloned.1.call-done = f32[80,768]{1,0:T(8,128)} async-done(((f32[1280,768]{1,0:T(8,128)}), f32[80,768]{1,0:T(8,128)}) %reduce-scatter.3.cloned.1.call-update) | async-done | bytes 245776 | tf_op jit(solution)/shard_map/reduce_scatter | solution.py:26
  420.0 1.6 add_convert_fusion
  (11 shorter events, 0.0 us)
Async XLA Ops:
  7.2 58.4 %copy-start = (bf16[768,1536]{1,0:T(8,128)(2,1)S(1)}, bf16[768,1536]{1,0:T(8,128)(2,1)}, u32[]{:S(2)}) copy-start(bf16[768,1536]{1,0:T(8,128)(2,1)} %param.7) | copy-start | bytes 7077892
  7.2 58.4 %all-gather.2.cloned.1.call-start = ((), (), s32[]{:S(2)}) async-start(), calls=%async_computation.3 | async-start | bytes 2088960 | tf_op jit(solution)/shard_map/all_gather | solution.py:15
  7.9 237.7 %all-reduce.3.cloned.1.call-start = ((), (), s32[]{:S(2)}) async-start(), calls=%async_computation.6 | async-start | bytes 31457280 | tf_op jit(solution)/shard_map/psum | solution.py:21
  8.0 39.2 %copy-start.7 = (bf16[1536,768]{1,0:T(8,128)(2,1)S(1)}, bf16[1536,768]{1,0:T(8,128)(2,1)}, u32[]{:S(2)}) copy-start(bf16[1536,768]{1,0:T(8,128)(2,1)} %param.9) | copy-start | bytes 7077892
  45.9 1.3 copy-start.2
  72.5 173.1 %copy-start.5 = (f32[1536]{0:T(1024)S(1)}, f32[1536]{0:T(1024)}, u32[]{:S(2)}) copy-start(f32[1536]{0:T(1024)} %param.8) | copy-start | bytes 18436
  72.6 267.9 %reduce-scatter.5.cloned.1.call-start = ((), (), s32[]{:S(2)}) async-start(), calls=%async_computation.5 | async-start | bytes 4177920 | tf_op jit(solution)/shard_map/reduce_scatter | solution.py:42
  256.3 1.9 copy-start.4
  263.3 1.7 copy-start.8
  263.3 156.6 %reduce-scatter.3.cloned.1.call-start = ((), (), s32[]{:S(2)}) async-start(), calls=%async_computation.4 | async-start | bytes 4177920 | tf_op jit(solution)/shard_map/reduce_scatter | solution.py:26
  272.2 1.6 copy-start.3
  289.0 130.9 %copy-start.6 = (f32[768]{0:T(1024)S(1)}, f32[768]{0:T(1024)}, u32[]{:S(2)}) copy-start(f32[768]{0:T(1024)} %param.10) | copy-start | bytes 9220
  289.0 132.5 %copy-start.1 = (bf16[768,1536]{1,0:T(8,128)(2,1)S(1)}, bf16[768,1536]{1,0:T(8,128)(2,1)}, u32[]{:S(2)}) copy-start(bf16[768,1536]{1,0:T(8,128)(2,1)} %param.7) | copy-start | bytes 7077892
Sparse Core Ops, SparseCore 0:
  10.2 55.3 all-gather.1
  72.7 172.8 all-reduce.2
  263.5 76.9 reduce-scatter.4
  343.7 76.2 reduce-scatter.2
